TPU v7x, 128 devices: a whole 4x4x4 slice. The times are simulated.
128 devices in a mesh: context: 32 (over y, z, core), tensor: 4 (over x).
Axes of the slice: x: 4, y: 4, z: 4, core: 2. Of those that a mesh axis runs over, the one named last changes fastest.
Arguments:
- mixer_input: bfloat16 [8192, 8192], P('context', 'tensor'), may hold values from -6 to 6
- step_raw: float32 [8192, 128], P('context', 'tensor'), may hold values from -3 to 3
- step_bias: float32 [128], P('tensor'), may hold values from -1 to 0.5
- decay_log: float32 [128], P('tensor'), may hold values from -14 to -3
- skip_gain: float32 [128], P('tensor'), may hold values from 0.5 to 1.5
- write_keys: bfloat16 [8192, 1024], P('context', 'tensor'), may hold values from -0.125 to 0.125
- read_keys: bfloat16 [8192, 1024], P('context', 'tensor'), may hold values from -0.375 to 0.375
- document_ids: int32 [8192], P('context'), may hold values from 0 to 2, never falling along the last dimension, each value on 1 to 4096 neighbouring positions
- query_rows: bfloat16 [8192, 4096], P('context', 'tensor'), may hold values from -128 to 128
- key_rows: bfloat16 [8192, 512], P(('context', 'tensor')), may hold values from -6 to 6
- value_rows: bfloat16 [8192, 512], P(('context', 'tensor')), may hold values from -6 to 6
Outputs:
- mixer_output: bfloat16 [8192, 8192], P('context', 'tensor')
- attention_output: bfloat16 [8192, 4096], P('context', 'tensor')
Inputs may be any that keep to these rules, and one draw needn't show every extreme that they name: `document_ids`: never falling along the sequence; one document holds exactly 4096 tokens.
All inputs are finite; a program needn't handle non-finite values.
Results may differ from a plain program's by a relative error of at most 0.011.
Values may be sent and summed in bfloat16 or wider, within the bound.
No kernel may reach another device: no remote copies, remote signals or barrier semaphores. Data moves between devices by JAX's collectives and lax.ppermute only.
A program may use at most 192 MiB of HBM per device.

v0:
```python
import functools
import math

import jax
import jax.numpy as jnp
from jax import lax
from jax.experimental import pallas as pl
from jax.experimental.pallas import tpu as pltpu
from jax.sharding import PartitionSpec as P

TOKENS = 256
HEADS = 32
WIDTH = 64
DSTATE = 256
REPEATS = 8
DIM = 128
META = 16
ROWS = TOKENS + META
HALF = HEADS * WIDTH // 2
QUARTER = HALF // 4
CHUNK = 2 * TOKENS
BLOCKS = 32
LEAD = 3

f32 = jnp.float32
bf16 = jnp.bfloat16
highest = lax.Precision.HIGHEST
negative = -1e30


def context_place():
    position = lax.axis_index("context")
    return position // 8, (position // 2) % 4, position % 2


def run(
    kernel, name, outs, *args, far=(), onto=None, scratch=(), mib=16, flops=0, transcendentals=0
):
    moved = sum(math.prod(a.shape) * a.dtype.itemsize for a in args)
    moved += sum(math.prod(a.shape) * a.dtype.itemsize for a in outs)
    spaces = [pltpu.HBM if number in far else pltpu.VMEM for number in range(len(args))]
    return pl.pallas_call(
        kernel,
        out_shape=outs,
        in_specs=[pl.BlockSpec(memory_space=space) for space in spaces],
        out_specs=[pl.BlockSpec(memory_space=pltpu.VMEM if onto is None else pltpu.HBM)] * len(outs),
        input_output_aliases={onto: 0} if onto is not None and onto >= 0 else {},
        scratch_shapes=list(scratch),
        compiler_params=pltpu.CompilerParams(vmem_limit_bytes=mib << 20),
        cost_estimate=pl.CostEstimate(
            flops=flops, bytes_accessed=moved, transcendentals=transcendentals
        ),
        name=name,
    )(*args)


def shape(rows, columns, dtype=bf16):
    return jax.ShapeDtypeStruct((rows, columns), dtype)


def iota(rows, columns, axis):
    return lax.broadcasted_iota(jnp.int32, (rows, columns), axis)


def split3(value):
    high = value.astype(bf16)
    rest = value - high.astype(f32)
    middle = rest.astype(bf16)
    low = (rest - middle.astype(f32)).astype(bf16)
    return high, middle, low


def spread_matrix(chunk, offset=0):
    column = iota(2 * HEADS, 256, 1) + 256 * chunk + offset
    return (column // WIDTH == iota(2 * HEADS, 256, 0) % HEADS).astype(bf16)


def two_parts(value):
    high, middle, _ = split3(value)
    return jnp.concatenate([high, middle], axis=1)


def spread(parts, matrix):
    return jnp.dot(parts, matrix, preferred_element_type=f32)


def document_column(docs_row):
    return jnp.broadcast_to(docs_row.astype(f32), (128, TOKENS)).T


def fetch(sources, targets, semaphores):
    copies = [
        pltpu.make_async_copy(source, target, semaphores.at[number])
        for number, (source, target) in enumerate(zip(sources, targets))
    ]
    for copy in copies:
        copy.start()
    return copies


def write_kernel(*refs):
    far, (mine, theirs, cum_out, offset_out), held, semaphores = refs[:6], refs[6:10], refs[10:16], refs[16]
    copies = fetch(far, held, semaphores)
    raw, bias, decay, docs, inputs, writes = held
    _, _, core = context_place()
    for copy in copies[:4]:
        copy.wait()
    padded = jnp.concatenate([raw[...], jnp.zeros((128 - HEADS, TOKENS), f32)], axis=0)
    u = padded.T[:, :HEADS] + bias[...]
    step = jnp.maximum(u, 0.0) + jnp.log1p(jnp.exp(-jnp.abs(u)))
    logdec = -step * jnp.exp(decay[...])
    triangle = (iota(TOKENS, TOKENS, 0) >= iota(TOKENS, TOKENS, 1)).astype(f32)
    cum = jnp.dot(triangle, logdec, precision=highest, preferred_element_type=f32)
    cum_out[...] = cum
    offset = cum - jnp.log(step)
    padded = jnp.concatenate([offset, jnp.zeros((TOKENS, 128 - HEADS), f32)], axis=1)
    offset_out[...] = padded.T[:HEADS]
    total = cum[TOKENS - 1 :]
    column = document_column(docs[...])[:, :HEADS]
    last = column[TOKENS - 1 :]
    trail = jnp.where(column == last, jnp.exp(total - cum), 0.0) * step
    high, middle, low = [part.astype(f32) for part in split3(total)]
    row = iota(META, HEADS, 0)
    meta = jnp.where(
        row == 0,
        high,
        jnp.where(row == 1, middle, jnp.where(row == 2, low, jnp.where(row == 3, last, 0.0))),
    ).astype(bf16)
    copies[5].wait()
    turned = writes[...].T
    copies[4].wait()
    matrices = [spread_matrix(chunk) for chunk in range(8)]
    trail = two_parts(trail)
    wide = [spread(trail, matrix) for matrix in matrices]
    scaled = [
        (inputs[:, 256 * chunk : 256 * (chunk + 1)].astype(f32) * wide[chunk]).astype(bf16)
        for chunk in range(8)
    ]
    states = [
        jnp.dot(turned, part, preferred_element_type=f32).astype(bf16) for part in scaled
    ]
    notes = [
        jnp.dot(meta, matrix[:HEADS], preferred_element_type=f32).astype(bf16) for matrix in matrices
    ]
    for chunk in range(4):
        columns = slice(256 * chunk, 256 * (chunk + 1))
        for rows, parts in ((slice(0, TOKENS), states), (slice(TOKENS, ROWS), notes)):
            mine[rows, columns] = jnp.where(core == 0, parts[chunk], parts[chunk + 4])
            theirs[rows, columns] = jnp.where(core == 0, parts[chunk + 4], parts[chunk])


def inside_kernel(cum, offset, docs, inputs, writes, reads, gain, out):
    scores = lax.dot_general(
        reads[...], writes[...], (((1,), (1,)), ((), ())), preferred_element_type=f32
    )
    column = document_column(docs[...])
    column = jnp.concatenate([column, column], axis=1)
    linked = (column == docs[...].astype(f32)) & (
        iota(TOKENS, TOKENS, 0) >= iota(TOKENS, TOKENS, 1)
    )
    scores = jnp.where(linked, scores, 0.0)
    upper = scores[:128, :128]
    lower = scores[128:]
    left = iota(TOKENS, 128, 1) < WIDTH
    for pair in range(HEADS // 2):
        columns = slice(128 * pair, 128 * (pair + 1))
        u = inputs[:, columns]
        zero = jnp.zeros_like(u)
        top = bottom = None
        for side in range(2):
            head = 2 * pair + side
            part = jnp.where(left, u, zero) if side == 0 else jnp.where(left, zero, u)
            ci = cum[:, head : head + 1]
            cj = offset[head : head + 1, :]
            first = (jnp.exp(ci[:128] - cj[:, :128]) * upper).astype(bf16)
            second = (jnp.exp(ci[128:] - cj) * lower).astype(bf16)
            first = jnp.dot(first, part[:128], preferred_element_type=f32)
            second = jnp.dot(second, part, preferred_element_type=f32)
            top = first if top is None else top + first
            bottom = second if bottom is None else bottom + second
        gains = jnp.where(
            left[:1], gain[:, 2 * pair : 2 * pair + 1], gain[:, 2 * pair + 1 : 2 * pair + 2]
        )
        wide = u.astype(f32) * gains
        out[:128, columns] = top + wide[:128]
        out[128:, columns] = bottom + wide[128:]


def described(ref_rows):
    rows = ref_rows.astype(f32)
    return rows[0:1] + rows[1:2] + rows[2:3], rows[3:4]


def meta_rows(total, last):
    high, middle, low = [part.astype(f32) for part in split3(total)]
    row = iota(META, total.shape[1], 0)
    return jnp.where(
        row == 0,
        high,
        jnp.where(row == 1, middle, jnp.where(row == 2, low, jnp.where(row == 3, last, 0.0))),
    ).astype(bf16)


def joined(earlier, later):
    total = earlier[1] + later[1]
    keep = jnp.where(later[2] == earlier[2], jnp.exp(later[1]), 0.0)
    return keep * earlier[0] + later[0], total, later[2]


def unpacked(payload):
    total, last = described(payload[TOKENS:])
    return payload[:TOKENS].astype(f32), total, last


def chip_kernel(mine, other, *outs):
    _, z, core = context_place()
    for step in range(4):
        columns = pl.ds(pl.multiple_of(((z + step) % 4) * QUARTER, QUARTER), QUARTER)
        own, near = mine[:, columns], other[:, columns]
        first = unpacked(jnp.where(core == 0, own, near))
        second = unpacked(jnp.where(core == 0, near, own))
        state, total, last = joined(first, second)
        outs[step][:TOKENS] = state.astype(bf16)
        outs[step][TOKENS:] = meta_rows(total, last)


def picked(slots, index):
    value = slots[0]
    for number in range(1, len(slots)):
        value = jnp.where(index == number, slots[number], value)
    return value


def row_kernel(a0, a1, a2, a3, out):
    _, z, _ = context_place()
    slots = [ref[...] for ref in (a0, a1, a2, a3)]
    whole = unpacked(picked(slots, z))
    for chip in range(1, 4):
        whole = joined(whole, unpacked(picked(slots, (z - chip) % 4)))
    out[:TOKENS] = whole[0].astype(bf16)
    out[TOKENS:] = meta_rows(whole[1], whole[2])


def entering_kernel(a0, a1, a2, a3, near, far, *outs):
    _, z, _ = context_place()
    slots = [ref[...] for ref in (a0, a1, a2, a3)]
    current = joined(unpacked(far[...]), unpacked(near[...]))
    entering = []
    for chip in range(4):
        entering.append((current[0].astype(bf16), meta_rows(current[1], current[2])))
        if chip < 3:
            current = joined(current, unpacked(picked(slots, (z - chip) % 4)))
    for step in range(4):
        outs[step][:TOKENS] = picked([e[0] for e in entering], (z + step) % 4)
        outs[step][TOKENS:] = picked([e[1] for e in entering], (z + step) % 4)


def core_kernel(b0, b1, b2, b3, mine, other, keep, send):
    _, z, core = context_place()
    for step, ref in enumerate((b0, b1, b2, b3)):
        columns = pl.ds(pl.multiple_of(((z - step) % 4) * QUARTER, QUARTER), QUARTER)
        first = ref[...]
        written = unpacked(jnp.where(core == 0, mine[:, columns], other[:, columns]))
        state, total, last = joined(unpacked(first), written)
        second = jnp.concatenate([state.astype(bf16), meta_rows(total, last)], axis=0)
        keep[:, columns] = jnp.where(core == 0, first, second)
        send[:, columns] = jnp.where(core == 0, second, first)


def carried_kernel(part, inside, cum, docs, reads, keep, state, *refs):
    out, held, semaphores = refs[part:]
    _, _, core = context_place()
    before = keep[TOKENS:, :HEADS][3:4].astype(f32)
    column = document_column(docs[...])[:, :HEADS]
    factor = two_parts(jnp.where(column == before, jnp.exp(cum[...]), 0.0))
    half = core if part == 0 else 1 - core
    offset = pl.multiple_of(half * HALF, HALF)
    carried = [
        jnp.dot(
            reads[...],
            state[:TOKENS, 256 * chunk : 256 * (chunk + 1)],
            preferred_element_type=f32,
        )
        for chunk in range(4)
    ]
    scale = [spread(factor, spread_matrix(chunk, offset)) for chunk in range(4)]
    copies = []
    for chunk in range(4):
        columns = pl.ds(pl.multiple_of(offset + 256 * chunk, 256), 256)
        local = slice(256 * chunk, 256 * (chunk + 1))
        result = inside[:, columns] + carried[chunk] * scale[chunk]
        held[:, local] = result.astype(bf16)
        copies += fetch([held.at[:, local]], [out.at[:, columns]], semaphores.at[pl.ds(chunk, 1)])
    for copy in copies:
        copy.wait()


def cut_kernel(keys, values, *refs):
    outs, semaphores = refs[:4], refs[4]
    x = lax.axis_index("tensor")
    sources, targets = [], []
    for step in range(4):
        columns = pl.ds(pl.multiple_of(((x + step) % 4) * DIM, DIM), DIM)
        sources += [keys.at[:, columns], values.at[:, columns]]
        targets += [outs[step].at[:, :DIM], outs[step].at[:, DIM:]]
    for copy in fetch(sources, targets, semaphores):
        copy.wait()


def assemble_kernel(p0, p1, p2, p3, docs, out):
    x = lax.axis_index("tensor")
    for step, ref in enumerate((p0, p1, p2, p3)):
        out[pl.ds(pl.multiple_of(((x - step) % 4) * 64, 64), 64), :] = ref[...]
    first = jnp.sum(jnp.where(docs[...] >= 1, 1.0, 0.0), axis=1, keepdims=True)
    second = jnp.sum(jnp.where(docs[...] >= 2, 1.0, 0.0), axis=1, keepdims=True)
    lane = iota(META, 2 * DIM, 1)
    counts = jnp.where(lane == 1, first, jnp.where(lane == 2, second, 0.0))
    out[TOKENS:] = jnp.where(lane == 0, float(TOKENS), counts).astype(bf16)


def chunk_kernel(mine, other, out):
    _, _, core = context_place()
    out[:ROWS] = jnp.where(core == 0, mine[...], other[...])
    out[ROWS:] = jnp.where(core == 0, other[...], mine[...])


def far_kernel(chunk, above, *outs):
    _, z, core = context_place()
    for step in range(1, 4):
        own = (core == 1) & ((z + step) % 4 > z)
        outs[step - 1][...] = jnp.where(own, chunk[...], above[...])


def bundle_kernel(a0, a1, a2, a3, out):
    for step, ref in enumerate((a0, a1, a2, a3)):
        out[2 * ROWS * step : 2 * ROWS * (step + 1)] = ref[...]


def chunk_of(blocks):
    one, two = blocks
    keys = jnp.concatenate([one[:, :DIM], two[:, :DIM]], axis=0)
    values = jnp.concatenate([one[:, DIM:], two[:, DIM:]], axis=0)
    values = jnp.concatenate([values.T, jnp.ones((META, CHUNK), bf16)], axis=0)
    return jnp.concatenate([keys, keys], axis=1), values


def mask_of(chunk, token, lowest):
    place = chunk * CHUNK + iota(CHUNK, TOKENS, 0)
    return jnp.where((place <= token) & (place >= lowest), 0.0, negative)


def fold(keys, values, bias, turned, peaks, sums, kind):
    def score(head):
        scores = jnp.dot(keys, turned[head], preferred_element_type=f32)
        return scores if bias is None else scores + bias

    def add(head, weights, shrink):
        new = jnp.dot(values, weights, preferred_element_type=f32)
        if kind == "first":
            sums[head] = new
        elif kind == "fixed":
            sums[head] = sums[head] + new
        else:
            sums[head] = sums[head] * shrink + new

    ahead = [score(head) for head in range(LEAD)]
    pending = None
    for head in range(REPEATS):
        if head + LEAD < REPEATS:
            ahead.append(score(head + LEAD))
        scores = ahead[head]
        shrink = None
        if kind == "fixed":
            new = peaks[head : head + 1]
        else:
            new = jnp.max(scores, axis=0, keepdims=True)
            if kind == "online":
                old = peaks[head : head + 1]
                new = jnp.maximum(old, new)
                shrink = jnp.exp2(old - new)
            peaks[head : head + 1] = new
        weights = jnp.exp2(scores - new).astype(bf16)
        if pending is not None:
            add(*pending)
        pending = (head, weights, shrink)
    add(*pending)


def starts_of(ids, start, base):
    below_one = jnp.sum(jnp.where(ids < 1, 1.0, 0.0)).astype(jnp.int32)
    below_two = jnp.sum(jnp.where(ids < 2, 1.0, 0.0)).astype(jnp.int32)
    opening = jnp.min(ids)
    return jnp.where(ids == opening, start, base + jnp.where(ids == 1, below_one, below_two))


def counted(counts, opening):
    here = (iota(META, 128, 0) == 0) & (iota(META, 128, 1) == opening)
    return jnp.sum(jnp.where(here, counts, 0.0)).astype(jnp.int32)


def own_kernel(queries, docs, chunk_ref, turned, peaks, sums):
    y, z, core = context_place()
    base = lax.axis_index("context") * TOKENS
    ids = docs[...]
    earlier = jnp.where(core == 1, chunk_ref[TOKENS:ROWS, :128].astype(f32), 0.0)
    lowest = starts_of(ids, base - counted(earlier, jnp.min(ids)), base)
    factor = math.log2(math.e) / math.sqrt(DIM)
    for head in range(REPEATS):
        scaled = (queries[:, head * DIM : (head + 1) * DIM].astype(f32) * factor).T
        high, middle, _ = split3(scaled)
        turned[head, :DIM] = high
        turned[head, DIM:] = middle
    bias = mask_of(y * 4 + z, base + iota(1, TOKENS, 1), lowest)
    keys, values = chunk_of([chunk_ref[:TOKENS], chunk_ref[ROWS : ROWS + TOKENS]])
    fold(keys, values, bias, turned, peaks, sums, "first")


def attention_kernel(docs, chunk_ref, bundle, arrived, turned, own_peaks, own_sums, out, peaks, sums):
    sums[...] = own_sums[...]
    y, z, core = context_place()
    base = lax.axis_index("context") * TOKENS
    own = y * 4 + z
    ids = docs[...]
    counts = jnp.where(core == 1, chunk_ref[TOKENS:ROWS, :128].astype(f32), 0.0)
    for block in range(8):
        rows = slice(block * ROWS + TOKENS, (block + 1) * ROWS)
        counts = counts + bundle[rows, :128].astype(f32) + arrived[rows, :128].astype(f32)
    start = base - counted(counts, jnp.min(ids))
    lowest = starts_of(ids, start, base)
    token = base + iota(1, TOKENS, 1)

    def visit(chunk, masked, peaks, kind):
        near = chunk // 4 == y - 1
        slot = ((z - chunk) % 4) * 2 * ROWS
        blocks = []
        for block in range(2):
            place = pl.ds(pl.multiple_of(slot + block * ROWS, ROWS), TOKENS)
            blocks.append(jnp.where(near == (core == 0), bundle[place, :], arrived[place, :]))
        keys, values = chunk_of(blocks)
        bias = mask_of(chunk, token, lowest) if masked else None
        fold(keys, values, bias, turned, peaks, sums, kind)

    first = start // CHUNK
    clear = jnp.minimum((jnp.max(lowest) + CHUNK - 1) // CHUNK, own)

    @pl.loop(first, clear)
    def _(chunk):
        visit(chunk, True, own_peaks, "fixed")

    @pl.loop(clear, own)
    def _(chunk):
        visit(chunk, False, own_peaks, "fixed")

    worst = jnp.max(jnp.concatenate([sums[head, DIM : DIM + 1] for head in range(REPEATS)], axis=0))

    @pl.when(jnp.logical_not(worst < 1e30))
    def _():
        peaks[...] = own_peaks[...]
        sums[...] = own_sums[...]

        @pl.loop(first, own)
        def _(chunk):
            visit(chunk, True, peaks, "online")

    for head in range(REPEATS):
        result = sums[head, :DIM] * (1.0 / sums[head, DIM : DIM + 1])
        out[:, head * DIM : (head + 1) * DIM] = result.T.astype(bf16)


def around_z(steps):
    return [
        (y * 8 + z * 2 + k, y * 8 + ((z + steps) % 4) * 2 + k)
        for y in range(4)
        for z in range(4)
        for k in range(2)
    ]


def along_y(steps):
    return [(c, c + 8 * steps) for c in range(BLOCKS - 8 * steps)]


def body(
    mixer_input,
    step_raw,
    step_bias,
    decay_log,
    skip_gain,
    write_keys,
    read_keys,
    document_ids,
    query_rows,
    key_rows,
    value_rows,
):
    docs = document_ids.reshape(1, TOKENS)
    across = [(c, c ^ 1) for c in range(BLOCKS)]
    below = [(c, c + 8 * (1 + c % 2)) for c in range(BLOCKS) if c + 8 * (1 + c % 2) < BLOCKS]

    cuts = run(
        cut_kernel,
        "cut_keys",
        [shape(64, 2 * DIM)] * 4,
        key_rows,
        value_rows,
        far=(0, 1),
        scratch=[pltpu.SemaphoreType.DMA((8,))],
        mib=56,
    )
    parts = [cuts[0]] + [
        lax.ppermute(cuts[step], "tensor", [(x, (x + step) % 4) for x in range(4)])
        for step in (1, 2, 3)
    ]

    mine, theirs, cum, offset = run(
        write_kernel,
        "mixer_write",
        [shape(ROWS, HALF), shape(ROWS, HALF), shape(TOKENS, HEADS, f32), shape(HEADS, TOKENS, f32)],
        step_raw.T,
        step_bias.reshape(1, HEADS),
        decay_log.reshape(1, HEADS),
        docs,
        mixer_input,
        write_keys,
        far=range(6),
        scratch=[
            pltpu.VMEM((HEADS, TOKENS), f32),
            pltpu.VMEM((1, HEADS), f32),
            pltpu.VMEM((1, HEADS), f32),
            pltpu.VMEM((1, TOKENS), jnp.int32),
            pltpu.VMEM((TOKENS, HEADS * WIDTH), bf16),
            pltpu.VMEM((TOKENS, DSTATE), bf16),
            pltpu.SemaphoreType.DMA((6,)),
        ],
        mib=56,
        flops=2 * 256 * 256 * 2048,
    )
    parts, mine, theirs, cum, offset = lax.optimization_barrier((parts, mine, theirs, cum, offset))
    (block,) = run(assemble_kernel, "assemble_keys", [shape(ROWS, 2 * DIM)], *parts, docs)
    other_block = lax.ppermute(block, "context", across)
    other = lax.ppermute(theirs, "context", across)

    quarter = [shape(ROWS, QUARTER)]
    (chunk,) = run(chunk_kernel, "chunk_keys", [shape(2 * ROWS, 2 * DIM)], block, other_block)
    above = lax.ppermute(chunk, "context", below)
    other, chunk = lax.optimization_barrier((other, chunk))
    chips = run(chip_kernel, "chip_state", quarter * 4, mine, other)
    slots = [chips[0]] + [lax.ppermute(chips[s], "context", around_z(s)) for s in (1, 2, 3)]

    (inside,) = run(
        inside_kernel,
        "mixer_inside",
        [shape(TOKENS, HEADS * WIDTH, f32)],
        cum,
        offset,
        docs,
        mixer_input,
        write_keys,
        read_keys,
        skip_gain.reshape(1, HEADS),
        mib=24,
        flops=2 * 256 * 256 * 128 * 32,
    )

    above, inside = lax.optimization_barrier((above, inside))
    far_cuts = run(far_kernel, "far_keys", [shape(2 * ROWS, 2 * DIM)] * 3, chunk, above)
    far = [lax.ppermute(far_cuts[s - 1], "context", around_z(s)) for s in (1, 2, 3)]

    slots, far_cuts = lax.optimization_barrier((slots, far_cuts))
    (row,) = run(row_kernel, "row_state", quarter, *slots)
    near_row = lax.ppermute(row, "context", along_y(1))
    far_row = lax.ppermute(row, "context", along_y(2))
    turned, peaks, sums = run(
        own_kernel,
        "attention_own",
        [
            jax.ShapeDtypeStruct((REPEATS, 2 * DIM, TOKENS), bf16),
            shape(REPEATS, TOKENS, f32),
            jax.ShapeDtypeStruct((REPEATS, DIM + META, TOKENS), f32),
        ],
        query_rows,
        docs,
        chunk,
        mib=24,
        flops=4 * 2048 * 512 * 128,
        transcendentals=2048 * 512,
    )
    near_row, far_row, turned = lax.optimization_barrier((near_row, far_row, turned))
    entering = run(entering_kernel, "entering_state", quarter * 4, *slots, near_row, far_row)
    back = [entering[0]] + [lax.ppermute(entering[s], "context", around_z(s)) for s in (1, 2, 3)]

    far, entering = lax.optimization_barrier((far, entering))
    (bundle,) = run(bundle_kernel, "bundle_keys", [shape(8 * ROWS, 2 * DIM)], above, *far)
    arrived = lax.ppermute(bundle, "context", across)

    (attended,) = run(
        attention_kernel,
        "attention",
        [shape(TOKENS, REPEATS * DIM)],
        docs,
        chunk,
        bundle,
        arrived,
        turned,
        peaks,
        sums,
        scratch=[
            pltpu.VMEM((REPEATS, TOKENS), f32),
            pltpu.VMEM((REPEATS, DIM + META, TOKENS), f32),
        ],
        mib=32,
        flops=4 * 2048 * 4096 * 128,
        transcendentals=2048 * 4096,
    )
    back, attended = lax.optimization_barrier((back, attended))

    keep, send = run(core_kernel, "core_state", [shape(ROWS, HALF)] * 2, *back, mine, other)
    state_arrived = lax.ppermute(send, "context", across)
    (own_half,) = run(
        functools.partial(carried_kernel, 0),
        "mixer_carried_own",
        [shape(TOKENS, HEADS * WIDTH)],
        inside,
        cum,
        docs,
        read_keys,
        keep,
        keep,
        onto=-1,
        scratch=[pltpu.VMEM((TOKENS, HALF), bf16), pltpu.SemaphoreType.DMA((4,))],
        mib=24,
        flops=2 * 256 * 256 * 1024,
    )
    state_arrived, own_half = lax.optimization_barrier((state_arrived, own_half))
    (mixed,) = run(
        functools.partial(carried_kernel, 1),
        "mixer_carried",
        [shape(TOKENS, HEADS * WIDTH)],
        inside,
        cum,
        docs,
        read_keys,
        keep,
        state_arrived,
        own_half,
        far=(6,),
        onto=6,
        scratch=[pltpu.VMEM((TOKENS, HALF), bf16), pltpu.SemaphoreType.DMA((4,))],
        mib=24,
        flops=2 * 256 * 256 * 1024,
    )
    return mixed, attended


def solution(mesh):
    placed = (
        P("context", "tensor"),
        P("context", "tensor"),
        P("tensor"),
        P("tensor"),
        P("tensor"),
        P("context", "tensor"),
        P("context", "tensor"),
        P("context"),
        P("context", "tensor"),
        P(("context", "tensor"), None),
        P(("context", "tensor"), None),
    )
    return jax.shard_map(
        body,
        mesh=mesh,
        in_specs=placed,
        out_specs=(P("context", "tensor"), P("context", "tensor")),
        check_vma=False,
    )
```

profile of v0, /device:TPU:1, one launch (start us, length us, event | category | flops | bytes accessed | tf_op | source)
XLA Modules:
  0.0 61.9 jit_solution(4433231555715070364)
XLA Ops:
  0.6 1.6 %cut_keys.1 = (bf16[64,256]{1,0:T(8,128)(2,1)}, bf16[64,256]{1,0:T(8,128)(2,1)}, bf16[64,256]{1,0:T(8,128)(2,1)}, bf16[64,256]{1,0:T(8,128)(2,1)}) custom-call(bf16[64,512]{1,0:T(8,128)(2,1)} %keys.1, bf16[64,512]{1,0:T(8,128)(2,1)} %values.1), custom_call_target="tpu_custom_call" | custom-call | bytes 262144 | tf_op jit(solution)/shard_map/cut_keys/pallas_call | solution.py:42
  2.2 2.1 %collective-permute-start = (bf16[64,256]{1,0:T(8,128)(2,1)}, bf16[64,256]{1,0:T(8,128)(2,1)S(1)}, u32[]{:S(2)}, u32[]{:S(2)}) collective-permute-start(bf16[64,256]{1,0:T(8,128)(2,1)} %get-tuple-element.56), channel_id=1, source_target_pairs={{0,1},{1,2},{2,3},{3,0},{4,5},{5,6},{6,7},{7,4},{8,9},{9,10},{10,1... | collective-permute-start | bytes 98312 | tf_op jit(solution)/shard_map/ppermute | solution.py:511
  4.3 2.5 %collective-permute-start.1 = (bf16[64,256]{1,0:T(8,128)(2,1)}, bf16[64,256]{1,0:T(8,128)(2,1)S(1)}, u32[]{:S(2)}, u32[]{:S(2)}) collective-permute-start(bf16[64,256]{1,0:T(8,128)(2,1)} %get-tuple-element.57), channel_id=1, source_target_pairs={{0,2},{1,3},{2,0},{3,1},{4,6},{5,7},{6,4},{7,5},{8,10},{9,11},{10,... | collective-permute-start | bytes 98312 | tf_op jit(solution)/shard_map/ppermute | solution.py:511
  6.8 1.2 %collective-permute-start.2 = (bf16[64,256]{1,0:T(8,128)(2,1)}, bf16[64,256]{1,0:T(8,128)(2,1)S(1)}, u32[]{:S(2)}, u32[]{:S(2)}) collective-permute-start(bf16[64,256]{1,0:T(8,128)(2,1)} %get-tuple-element.58), channel_id=1, source_target_pairs={{0,3},{1,0},{2,1},{3,2},{4,7},{5,4},{6,5},{7,6},{8,11},{9,8},{10,9... | collective-permute-start | bytes 98312 | tf_op jit(solution)/shard_map/ppermute | solution.py:511
  8.0 3.8 %mixer_write.1 = (bf16[272,1024]{1,0:T(8,128)(2,1)}, bf16[272,1024]{1,0:T(8,128)(2,1)}, f32[256,32]{1,0:T(8,128)}, f32[32,256]{1,0:T(8,128)}) custom-call(f32[32,256]{1,0:T(8,128)} %bitcast.13, f32[1,32]{1,0:T(1,128)} %bitcast.14, f32[1,32]{1,0:T(1,128)} %bitcast.15, s32[1,256]{1,0:T(1,128)} %bitcast.5, bf16[256,2048]{1,0:T(8,128)(2,1)} %inputs.1, ...), custom_call_target="tpu_custom_call" | custom-call | flops 268435456 | bytes 2393344 | tf_op jit(solution)/shard_map/mixer_write/pallas_call | solution.py:42
  11.8 1.6 %collective-permute-start.5 = (bf16[272,1024]{1,0:T(8,128)(2,1)}, bf16[272,1024]{1,0:T(8,128)(2,1)S(1)}, u32[]{:S(2)}, u32[]{:S(2)}) collective-permute-start(bf16[272,1024]{1,0:T(8,128)(2,1)} %get-tuple-element.71), channel_id=1, source_target_pairs={{0,4},{4,0},{8,12},{12,8},{16,20},{20,16},{24,28},{28,24},{32,36},... | collective-permute-start | bytes 1671176 | tf_op jit(solution)/shard_map/ppermute | solution.py:541
  13.5 1.6 %collective-permute-done.3.other = bf16[272,256]{1,0:T(8,128)(2,1)S(1)} collective-permute-done((bf16[272,256]{1,0:T(8,128)(2,1)S(1)}, bf16[272,256]{1,0:T(8,128)(2,1)S(1)}, u32[]{:S(2)}, u32[]{:S(2)}) %collective-permute-start.3) | collective-permute-done | bytes 139296 | tf_op jit(solution)/shard_map/ppermute | solution.py:540
  15.2 4.8 %collective-permute-start.4 = (bf16[544,256]{1,0:T(8,128)(2,1)S(1)}, bf16[544,256]{1,0:T(8,128)(2,1)S(1)}, u32[]{:S(2)}, u32[]{:S(2)}) collective-permute-start(bf16[544,256]{1,0:T(8,128)(2,1)S(1)} %chunk_keys.1.chunk.chunk_ref), channel_id=1, source_target_pairs={{0,32},{4,68},{8,40},{12,76},{16,48},{20,84},{24,56},{28,92},{32,6... | collective-permute-start | bytes 835592 | tf_op jit(solution)/shard_map/ppermute | solution.py:545
  20.0 1.0 %copy-done.1 = bf16[272,1024]{1,0:T(8,128)(2,1)S(1)} copy-done((bf16[272,1024]{1,0:T(8,128)(2,1)S(1)}, bf16[272,1024]{1,0:T(8,128)(2,1)}, u32[]{:S(2)}) %copy-start.1) | copy-done | bytes 557080
  21.3 1.7 %collective-permute-start.6 = (bf16[272,256]{1,0:T(8,128)(2,1)S(1)}, bf16[272,256]{1,0:T(8,128)(2,1)S(1)}, u32[]{:S(2)}, u32[]{:S(2)}) collective-permute-start(bf16[272,256]{1,0:T(8,128)(2,1)S(1)} %get-tuple-element.74), channel_id=1, source_target_pairs={{0,8},{4,12},{8,16},{12,20},{16,24},{20,28},{24,0},{28,4},{32,40},... | collective-permute-start | bytes 417800 | tf_op jit(solution)/shard_map/ppermute | solution.py:548
  23.0 3.3 %collective-permute-start.7 = (bf16[272,256]{1,0:T(8,128)(2,1)S(1)}, bf16[272,256]{1,0:T(8,128)(2,1)S(1)}, u32[]{:S(2)}, u32[]{:S(2)}) collective-permute-start(bf16[272,256]{1,0:T(8,128)(2,1)S(1)} %get-tuple-element.75), channel_id=1, source_target_pairs={{0,16},{4,20},{8,24},{12,28},{16,0},{20,4},{24,8},{28,12},{32,48},... | collective-permute-start | bytes 417800 | tf_op jit(solution)/shard_map/ppermute | solution.py:548
  27.9 2.2 %mixer_inside.1.inside = f32[256,2048]{1,0:T(8,128)S(1)} custom-call(f32[256,32]{1,0:T(8,128)S(1)} %copy-done.4, f32[32,256]{1,0:T(8,128)S(1)} %copy-done.6, s32[1,256]{1,0:T(1,128)S(1)} %bitcast.7, bf16[256,2048]{1,0:T(8,128)(2,1)S(1)} %copy-done, bf16[256,256]{1,0:T(8,128)(2,1)S(1)} %copy-done.5, bf16[256,256]{1,0:T(8,128)(2,1)S(1)} %copy-done.3, ...), custom_call_target="tpu_custom_call" | custom-call | flops 536870912 | bytes 3474560 | tf_op jit(solution)/shard_map/mixer_inside/pallas_call | solution.py:42
  31.4 2.0 %collective-permute-start.16 = (bf16[544,256]{1,0:T(8,128)(2,1)S(1)}, bf16[544,256]{1,0:T(8,128)(2,1)S(1)}, u32[]{:S(2)}, u32[]{:S(2)}) collective-permute-start(bf16[544,256]{1,0:T(8,128)(2,1)S(1)} %get-tuple-element.81), channel_id=1, source_target_pairs={{0,24},{4,28},{8,0},{12,4},{16,8},{20,12},{24,16},{28,20},{32,56},... | collective-permute-start | bytes 835592 | tf_op jit(solution)/shard_map/ppermute | solution.py:567
  33.7 3.7 %collective-permute-start.10 = (bf16[272,256]{1,0:T(8,128)(2,1)S(1)}, bf16[272,256]{1,0:T(8,128)(2,1)S(1)}, u32[]{:S(2)}, u32[]{:S(2)}) collective-permute-start(bf16[272,256]{1,0:T(8,128)(2,1)S(1)} %row_state.1), channel_id=1, source_target_pairs={{0,64},{4,68},{8,72},{12,76},{16,80},{20,84},{24,88},{28,92},{32,9... | collective-permute-start | bytes 417800 | tf_op jit(solution)/shard_map/ppermute | solution.py:572
  37.4 1.3 %collective-permute-start.9 = (bf16[272,256]{1,0:T(8,128)(2,1)S(1)}, bf16[272,256]{1,0:T(8,128)(2,1)S(1)}, u32[]{:S(2)}, u32[]{:S(2)}) collective-permute-start(bf16[272,256]{1,0:T(8,128)(2,1)S(1)} %row_state.1), channel_id=1, source_target_pairs={{0,32},{4,36},{8,40},{12,44},{16,48},{20,52},{24,56},{28,60},{32,6... | collective-permute-start | bytes 417800 | tf_op jit(solution)/shard_map/ppermute | solution.py:571
  38.7 1.8 %attention_own.1 = (bf16[8,256,256]{2,1,0:T(8,128)(2,1)S(1)}, f32[8,256]{1,0:T(8,128)S(1)}, f32[8,144,256]{2,1,0:T(8,128)S(1)}) custom-call(bf16[256,1024]{1,0:T(8,128)(2,1)S(1)} %copy-done.10, s32[1,256]{1,0:T(1,128)S(1)} %bitcast.8, bf16[544,256]{1,0:T(8,128)(2,1)S(1)} %chunk_keys.1.chunk.chunk_ref), custom_call_target="tpu_custom_call" | custom-call | flops 536870912 | bytes 3040256 | tf_op jit(solution)/shard_map/attention_own/pallas_call | solution.py:42
  40.5 1.6 %collective-permute-done.9.near = bf16[272,256]{1,0:T(8,128)(2,1)S(1)} collective-permute-done((bf16[272,256]{1,0:T(8,128)(2,1)S(1)}, bf16[272,256]{1,0:T(8,128)(2,1)S(1)}, u32[]{:S(2)}, u32[]{:S(2)}) %collective-permute-start.9) | collective-permute-done | bytes 139296 | tf_op jit(solution)/shard_map/ppermute | solution.py:571
  42.4 3.4 %collective-permute-done.14.a1 = bf16[544,256]{1,0:T(8,128)(2,1)S(1)} collective-permute-done((bf16[544,256]{1,0:T(8,128)(2,1)S(1)}, bf16[544,256]{1,0:T(8,128)(2,1)S(1)}, u32[]{:S(2)}, u32[]{:S(2)}) %collective-permute-start.14) | collective-permute-done | bytes 278560 | tf_op jit(solution)/shard_map/ppermute | solution.py:567
  46.2 1.0 %collective-permute-start.17 = (bf16[2176,256]{1,0:T(8,128)(2,1)S(1)}, bf16[2176,256]{1,0:T(8,128)(2,1)S(1)}, u32[]{:S(2)}, u32[]{:S(2)}) collective-permute-start(bf16[2176,256]{1,0:T(8,128)(2,1)S(1)} %bundle_keys.1.bundle), channel_id=1, source_target_pairs={{0,4},{4,0},{8,12},{12,8},{16,20},{20,16},{24,28},{28,24},{32,36},... | collective-permute-start | bytes 3342344 | tf_op jit(solution)/shard_map/ppermute | solution.py:594
  47.8 3.0 %collective-permute-start.12 = (bf16[272,256]{1,0:T(8,128)(2,1)S(1)}, bf16[272,256]{1,0:T(8,128)(2,1)S(1)}, u32[]{:S(2)}, u32[]{:S(2)}) collective-permute-start(bf16[272,256]{1,0:T(8,128)(2,1)S(1)} %get-tuple-element.91), channel_id=1, source_target_pairs={{0,16},{4,20},{8,24},{12,28},{16,0},{20,4},{24,8},{28,12},{32,48},... | collective-permute-start | bytes 417800 | tf_op jit(solution)/shard_map/ppermute | solution.py:590
  50.8 1.9 %attention.1 = bf16[256,1024]{1,0:T(8,128)(2,1)} custom-call(s32[1,256]{1,0:T(1,128)S(1)} %bitcast.9, bf16[544,256]{1,0:T(8,128)(2,1)S(1)} %chunk_keys.1.chunk.chunk_ref, bf16[2176,256]{1,0:T(8,128)(2,1)S(1)} %bundle_keys.1.bundle, bf16[2176,256]{1,0:T(8,128)(2,1)S(1)} %collective-permute-done.17.arrived, bf16[8,256,256]{2,1,0:T(8,128)(2,1)S(1)} %get-tuple-element.96.turned, ...), custom_call_target="tpu_custom_call" | custom-call | flops 4294967296 | bytes 5268480 | tf_op jit(solution)/shard_map/attention/pallas_call | solution.py:42
  53.7 3.8 %collective-permute-done.12.b2 = bf16[272,256]{1,0:T(8,128)(2,1)S(1)} collective-permute-done((bf16[272,256]{1,0:T(8,128)(2,1)S(1)}, bf16[272,256]{1,0:T(8,128)(2,1)S(1)}, u32[]{:S(2)}, u32[]{:S(2)}) %collective-permute-start.12) | collective-permute-done | bytes 139296 | tf_op jit(solution)/shard_map/ppermute | solution.py:590
  58.9 1.3 %mixer_carried_own.1.refs_0_ = bf16[256,2048]{1,0:T(8,128)(2,1)} custom-call(f32[256,2048]{1,0:T(8,128)S(1)} %mixer_inside.1.inside, f32[256,32]{1,0:T(8,128)S(1)} %copy-done.4, s32[1,256]{1,0:T(1,128)S(1)} %bitcast.10, bf16[256,256]{1,0:T(8,128)(2,1)S(1)} %copy-done.3, bf16[272,1024]{1,0:T(8,128)(2,1)S(1)} %get-tuple-element.103.keep.state, ...), custom_call_target="tpu_custom_call" | custom-call | flops 134217728 | bytes 4424704 | tf_op jit(solution)/shard_map/mixer_carried_own/pallas_call | solution.py:42
  60.4 1.3 %mixer_carried.1 = bf16[256,2048]{1,0:T(8,128)(2,1)} custom-call(f32[256,2048]{1,0:T(8,128)S(1)} %mixer_inside.1.inside, f32[256,32]{1,0:T(8,128)S(1)} %copy-done.4, s32[1,256]{1,0:T(1,128)S(1)} %bitcast.11, bf16[256,256]{1,0:T(8,128)(2,1)S(1)} %copy-done.3, bf16[272,1024]{1,0:T(8,128)(2,1)S(1)} %get-tuple-element.103.keep.state, ...), custom_call_target="tpu_custom_call", output_to_operand_aliasing={{}: (6, {})} | custom-call | flops 134217728 | bytes 5473280 | tf_op jit(solution)/shard_map/mixer_carried/pallas_call | solution.py:42
  (51 shorter events, 7.5 us)
Async XLA Ops:
  0.6 12.7 %copy-start.8 = (s32[256]{0:T(256)S(1)}, s32[256]{0:T(256)}, u32[]{:S(2)}) copy-start(s32[256]{0:T(256)} %param.18) | copy-start | bytes 3076
  2.2 9.5 %collective-permute-start = (bf16[64,256]{1,0:T(8,128)(2,1)}, bf16[64,256]{1,0:T(8,128)(2,1)S(1)}, u32[]{:S(2)}, u32[]{:S(2)}) collective-permute-start(bf16[64,256]{1,0:T(8,128)(2,1)} %get-tuple-element.56), channel_id=1, source_target_pairs={{0,1},{1,2},{2,3},{3,0},{4,5},{5,6},{6,7},{7,4},{8,9},{9,10},{10,1... | collective-permute-start | bytes 98312 | tf_op jit(solution)/shard_map/ppermute | solution.py:511
  4.3 7.4 %collective-permute-start.1 = (bf16[64,256]{1,0:T(8,128)(2,1)}, bf16[64,256]{1,0:T(8,128)(2,1)S(1)}, u32[]{:S(2)}, u32[]{:S(2)}) collective-permute-start(bf16[64,256]{1,0:T(8,128)(2,1)} %get-tuple-element.57), channel_id=1, source_target_pairs={{0,2},{1,3},{2,0},{3,1},{4,6},{5,7},{6,4},{7,5},{8,10},{9,11},{10,... | collective-permute-start | bytes 98312 | tf_op jit(solution)/shard_map/ppermute | solution.py:511
  6.8 5.0 %collective-permute-start.2 = (bf16[64,256]{1,0:T(8,128)(2,1)}, bf16[64,256]{1,0:T(8,128)(2,1)S(1)}, u32[]{:S(2)}, u32[]{:S(2)}) collective-permute-start(bf16[64,256]{1,0:T(8,128)(2,1)} %get-tuple-element.58), channel_id=1, source_target_pairs={{0,3},{1,0},{2,1},{3,2},{4,7},{5,4},{6,5},{7,6},{8,11},{9,8},{10,9... | collective-permute-start | bytes 98312 | tf_op jit(solution)/shard_map/ppermute | solution.py:511
  7.9 19.1 %copy-start.3 = (bf16[256,256]{1,0:T(8,128)(2,1)S(1)}, bf16[256,256]{1,0:T(8,128)(2,1)}, u32[]{:S(2)}) copy-start(bf16[256,256]{1,0:T(8,128)(2,1)} %reads.5) | copy-start | bytes 393220
  7.9 19.1 %copy-start.5 = (bf16[256,256]{1,0:T(8,128)(2,1)S(1)}, bf16[256,256]{1,0:T(8,128)(2,1)}, u32[]{:S(2)}) copy-start(bf16[256,256]{1,0:T(8,128)(2,1)} %writes.1) | copy-start | bytes 393220
  8.0 19.1 %copy-start.9 = (f32[32]{0:T(128)S(1)}, f32[32]{0:T(128)}, u32[]{:S(2)}) copy-start(f32[32]{0:T(128)} %param.15) | copy-start | bytes 388
  11.7 15.4 %copy-start = (bf16[256,2048]{1,0:T(8,128)(2,1)S(1)}, bf16[256,2048]{1,0:T(8,128)(2,1)}, u32[]{:S(2)}) copy-start(bf16[256,2048]{1,0:T(8,128)(2,1)} %inputs.1) | copy-start | bytes 3145732
  11.8 8.3 %collective-permute-start.5 = (bf16[272,1024]{1,0:T(8,128)(2,1)}, bf16[272,1024]{1,0:T(8,128)(2,1)S(1)}, u32[]{:S(2)}, u32[]{:S(2)}) collective-permute-start(bf16[272,1024]{1,0:T(8,128)(2,1)} %get-tuple-element.71), channel_id=1, source_target_pairs={{0,4},{4,0},{8,12},{12,8},{16,20},{20,16},{24,28},{28,24},{32,36},... | collective-permute-start | bytes 1671176 | tf_op jit(solution)/shard_map/ppermute | solution.py:541
  13.5 1.7 %collective-permute-start.3 = (bf16[272,256]{1,0:T(8,128)(2,1)S(1)}, bf16[272,256]{1,0:T(8,128)(2,1)S(1)}, u32[]{:S(2)}, u32[]{:S(2)}) collective-permute-start(bf16[272,256]{1,0:T(8,128)(2,1)S(1)} %assemble_keys.1.mine), channel_id=1, source_target_pairs={{0,4},{4,0},{8,12},{12,8},{16,20},{20,16},{24,28},{28,24},{32,36},... | collective-permute-start | bytes 417800 | tf_op jit(solution)/shard_map/ppermute | solution.py:540
  15.2 14.8 %collective-permute-start.4 = (bf16[544,256]{1,0:T(8,128)(2,1)S(1)}, bf16[544,256]{1,0:T(8,128)(2,1)S(1)}, u32[]{:S(2)}, u32[]{:S(2)}) collective-permute-start(bf16[544,256]{1,0:T(8,128)(2,1)S(1)} %chunk_keys.1.chunk.chunk_ref), channel_id=1, source_target_pairs={{0,32},{4,68},{8,40},{12,76},{16,48},{20,84},{24,56},{28,92},{32,6... | collective-permute-start | bytes 835592 | tf_op jit(solution)/shard_map/ppermute | solution.py:545
  21.3 10.1 %collective-permute-start.6 = (bf16[272,256]{1,0:T(8,128)(2,1)S(1)}, bf16[272,256]{1,0:T(8,128)(2,1)S(1)}, u32[]{:S(2)}, u32[]{:S(2)}) collective-permute-start(bf16[272,256]{1,0:T(8,128)(2,1)S(1)} %get-tuple-element.74), channel_id=1, source_target_pairs={{0,8},{4,12},{8,16},{12,20},{16,24},{20,28},{24,0},{28,4},{32,40},... | collective-permute-start | bytes 417800 | tf_op jit(solution)/shard_map/ppermute | solution.py:548
  23.0 10.4 %collective-permute-start.7 = (bf16[272,256]{1,0:T(8,128)(2,1)S(1)}, bf16[272,256]{1,0:T(8,128)(2,1)S(1)}, u32[]{:S(2)}, u32[]{:S(2)}) collective-permute-start(bf16[272,256]{1,0:T(8,128)(2,1)S(1)} %get-tuple-element.75), channel_id=1, source_target_pairs={{0,16},{4,20},{8,24},{12,28},{16,0},{20,4},{24,8},{28,12},{32,48},... | collective-permute-start | bytes 417800 | tf_op jit(solution)/shard_map/ppermute | solution.py:548
  26.3 7.1 %collective-permute-start.8 = (bf16[272,256]{1,0:T(8,128)(2,1)S(1)}, bf16[272,256]{1,0:T(8,128)(2,1)S(1)}, u32[]{:S(2)}, u32[]{:S(2)}) collective-permute-start(bf16[272,256]{1,0:T(8,128)(2,1)S(1)} %get-tuple-element.76), channel_id=1, source_target_pairs={{0,24},{4,28},{8,0},{12,4},{16,8},{20,12},{24,16},{28,20},{32,56},... | collective-permute-start | bytes 417800 | tf_op jit(solution)/shard_map/ppermute | solution.py:548
  30.2 15.6 %collective-permute-start.14 = (bf16[544,256]{1,0:T(8,128)(2,1)S(1)}, bf16[544,256]{1,0:T(8,128)(2,1)S(1)}, u32[]{:S(2)}, u32[]{:S(2)}) collective-permute-start(bf16[544,256]{1,0:T(8,128)(2,1)S(1)} %get-tuple-element.79), channel_id=1, source_target_pairs={{0,8},{4,12},{8,16},{12,20},{16,24},{20,28},{24,0},{28,4},{32,40},... | collective-permute-start | bytes 835592 | tf_op jit(solution)/shard_map/ppermute | solution.py:567
  31.0 14.8 %collective-permute-start.15 = (bf16[544,256]{1,0:T(8,128)(2,1)S(1)}, bf16[544,256]{1,0:T(8,128)(2,1)S(1)}, u32[]{:S(2)}, u32[]{:S(2)}) collective-permute-start(bf16[544,256]{1,0:T(8,128)(2,1)S(1)} %get-tuple-element.80), channel_id=1, source_target_pairs={{0,16},{4,20},{8,24},{12,28},{16,0},{20,4},{24,8},{28,12},{32,48},... | collective-permute-start | bytes 835592 | tf_op jit(solution)/shard_map/ppermute | solution.py:567
  31.4 14.7 %collective-permute-start.16 = (bf16[544,256]{1,0:T(8,128)(2,1)S(1)}, bf16[544,256]{1,0:T(8,128)(2,1)S(1)}, u32[]{:S(2)}, u32[]{:S(2)}) collective-permute-start(bf16[544,256]{1,0:T(8,128)(2,1)S(1)} %get-tuple-element.81), channel_id=1, source_target_pairs={{0,24},{4,28},{8,0},{12,4},{16,8},{20,12},{24,16},{28,20},{32,56},... | collective-permute-start | bytes 835592 | tf_op jit(solution)/shard_map/ppermute | solution.py:567
  33.7 6.8 %collective-permute-start.10 = (bf16[272,256]{1,0:T(8,128)(2,1)S(1)}, bf16[272,256]{1,0:T(8,128)(2,1)S(1)}, u32[]{:S(2)}, u32[]{:S(2)}) collective-permute-start(bf16[272,256]{1,0:T(8,128)(2,1)S(1)} %row_state.1), channel_id=1, source_target_pairs={{0,64},{4,68},{8,72},{12,76},{16,80},{20,84},{24,88},{28,92},{32,9... | collective-permute-start | bytes 417800 | tf_op jit(solution)/shard_map/ppermute | solution.py:572
  37.4 4.7 %collective-permute-start.9 = (bf16[272,256]{1,0:T(8,128)(2,1)S(1)}, bf16[272,256]{1,0:T(8,128)(2,1)S(1)}, u32[]{:S(2)}, u32[]{:S(2)}) collective-permute-start(bf16[272,256]{1,0:T(8,128)(2,1)S(1)} %row_state.1), channel_id=1, source_target_pairs={{0,32},{4,36},{8,40},{12,44},{16,48},{20,52},{24,56},{28,60},{32,6... | collective-permute-start | bytes 417800 | tf_op jit(solution)/shard_map/ppermute | solution.py:571
  46.2 4.6 %collective-permute-start.17 = (bf16[2176,256]{1,0:T(8,128)(2,1)S(1)}, bf16[2176,256]{1,0:T(8,128)(2,1)S(1)}, u32[]{:S(2)}, u32[]{:S(2)}) collective-permute-start(bf16[2176,256]{1,0:T(8,128)(2,1)S(1)} %bundle_keys.1.bundle), channel_id=1, source_target_pairs={{0,4},{4,0},{8,12},{12,8},{16,20},{20,16},{24,28},{28,24},{32,36},... | collective-permute-start | bytes 3342344 | tf_op jit(solution)/shard_map/ppermute | solution.py:594
  47.3 6.5 %collective-permute-start.11 = (bf16[272,256]{1,0:T(8,128)(2,1)S(1)}, bf16[272,256]{1,0:T(8,128)(2,1)S(1)}, u32[]{:S(2)}, u32[]{:S(2)}) collective-permute-start(bf16[272,256]{1,0:T(8,128)(2,1)S(1)} %get-tuple-element.90), channel_id=1, source_target_pairs={{0,8},{4,12},{8,16},{12,20},{16,24},{20,28},{24,0},{28,4},{32,40},... | collective-permute-start | bytes 417800 | tf_op jit(solution)/shard_map/ppermute | solution.py:590
  47.8 9.8 %collective-permute-start.12 = (bf16[272,256]{1,0:T(8,128)(2,1)S(1)}, bf16[272,256]{1,0:T(8,128)(2,1)S(1)}, u32[]{:S(2)}, u32[]{:S(2)}) collective-permute-start(bf16[272,256]{1,0:T(8,128)(2,1)S(1)} %get-tuple-element.91), channel_id=1, source_target_pairs={{0,16},{4,20},{8,24},{12,28},{16,0},{20,4},{24,8},{28,12},{32,48},... | collective-permute-start | bytes 417800 | tf_op jit(solution)/shard_map/ppermute | solution.py:590
  50.8 6.7 %collective-permute-start.13 = (bf16[272,256]{1,0:T(8,128)(2,1)S(1)}, bf16[272,256]{1,0:T(8,128)(2,1)S(1)}, u32[]{:S(2)}, u32[]{:S(2)}) collective-permute-start(bf16[272,256]{1,0:T(8,128)(2,1)S(1)} %get-tuple-element.92), channel_id=1, source_target_pairs={{0,24},{4,28},{8,0},{12,4},{16,8},{20,12},{24,16},{28,20},{32,56},... | collective-permute-start | bytes 417800 | tf_op jit(solution)/shard_map/ppermute | solution.py:590
  57.9 2.5 %collective-permute-start.18 = (bf16[272,1024]{1,0:T(8,128)(2,1)S(1)}, bf16[272,1024]{1,0:T(8,128)(2,1)S(1)}, u32[]{:S(2)}, u32[]{:S(2)}) collective-permute-start(bf16[272,1024]{1,0:T(8,128)(2,1)S(1)} %get-tuple-element.104), channel_id=1, source_target_pairs={{0,4},{4,0},{8,12},{12,8},{16,20},{20,16},{24,28},{28,24},{32,36},... | collective-permute-start | bytes 1671176 | tf_op jit(solution)/shard_map/ppermute | solution.py:618
  (6 other events, 34.4 us)
where the time goes:
time: 62.6 us; the launch traced here: 61.9 us
  starting transfers between devices  31.8 us (51%)
  Pallas kernels  15.1 us (24%)
  waiting for transfers between devices  12.2 us (19%)
  local copies, waits for them, and re-layouts  1.84 us (3%)
  between operations  1.02 us (2%)
    pallas_call x15, Pallas kernels, run(): pl.pallas_call(kernel, out_shape=outs, in_specs=[pl.BlockSpec(memory_spac...  15.1 us
    ppermute x3, starting transfers between devices, body(): lax.ppermute(chips[s], 'context', around_z(s))  5.74 us
    ppermute x3, starting transfers between devices, body(): lax.ppermute(cuts[step], 'tensor', [(x, (x + step) % 4) for x in range(4)])  5.71 us
    ppermute x3, waiting for transfers between devices, body(): lax.ppermute(entering[s], 'context', around_z(s))  4.88 us
    ppermute x1, starting transfers between devices, body(): above = lax.ppermute(chunk, 'context', below)  4.83 us
    ppermute x3, waiting for transfers between devices, body(): lax.ppermute(far_cuts[s - 1], 'context', around_z(s))  3.79 us
    ppermute x1, starting transfers between devices, body(): far_row = lax.ppermute(row, 'context', along_y(2))  3.7 us
    ppermute x3, starting transfers between devices, body(): lax.ppermute(entering[s], 'context', around_z(s))  3.55 us
  transfers between devices with their start and end apart: 19, of which 7 were waited for; matrix products, arithmetic and copies ran while one was open for 0% of the time, Pallas kernels for 19%

commit v1 on v0

--- a/solution.py
+++ b/solution.py
@@ -538,12 +538,12 @@
     parts, mine, theirs, cum, offset = lax.optimization_barrier((parts, mine, theirs, cum, offset))
     (block,) = run(assemble_kernel, "assemble_keys", [shape(ROWS, 2 * DIM)], *parts, docs)
     other_block = lax.ppermute(block, "context", across)
-    other = lax.ppermute(theirs, "context", across)
 
     quarter = [shape(ROWS, QUARTER)]
     (chunk,) = run(chunk_kernel, "chunk_keys", [shape(2 * ROWS, 2 * DIM)], block, other_block)
     above = lax.ppermute(chunk, "context", below)
-    other, chunk = lax.optimization_barrier((other, chunk))
+    theirs, chunk = lax.optimization_barrier((theirs, chunk))
+    other = lax.ppermute(theirs, "context", across)
     chips = run(chip_kernel, "chip_state", quarter * 4, mine, other)
     slots = [chips[0]] + [lax.ppermute(chips[s], "context", around_z(s)) for s in (1, 2, 3)]
 

time: 62.6 us -> 62 us (level)
    ppermute x1, starting transfers between devices: 0.06 us -> 1.54 us  [body(): other_block = lax.ppermute(block, 'context', across)]
    ppermute x1, starting transfers between devices: 1.59 us -> 0.44 us  [body(): other = lax.ppermute(theirs, 'context', across)]
    ppermute x1, waiting for transfers between devices: 1.63 us -> 1 us  [body(): other_block = lax.ppermute(block, 'context', across)]
where the time goes in v1:
time: 62 us; the launch traced here: 61.6 us
  starting transfers between devices  31.6 us (51%)
  Pallas kernels  15.1 us (24%)
  waiting for transfers between devices  12 us (19%)
  local copies, waits for them, and re-layouts  1.84 us (3%)
  between operations  1.03 us (2%)
    pallas_call x15, Pallas kernels, run(): pl.pallas_call(kernel, out_shape=outs, in_specs=[pl.BlockSpec(memory_spac...  15.1 us
    ppermute x3, starting transfers between devices, body(): lax.ppermute(chips[s], 'context', around_z(s))  5.74 us
    ppermute x3, starting transfers between devices, body(): lax.ppermute(cuts[step], 'tensor', [(x, (x + step) % 4) for x in range(4)])  5.71 us
    ppermute x3, waiting for transfers between devices, body(): lax.ppermute(entering[s], 'context', around_z(s))  4.88 us
    ppermute x1, starting transfers between devices, body(): above = lax.ppermute(chunk, 'context', below)  4.82 us
    ppermute x3, waiting for transfers between devices, body(): lax.ppermute(far_cuts[s - 1], 'context', around_z(s))  4.18 us
    ppermute x3, starting transfers between devices, body(): lax.ppermute(entering[s], 'context', around_z(s))  3.55 us
    ppermute x1, starting transfers between devices, body(): far_row = lax.ppermute(row, 'context', along_y(2))  3.53 us
  transfers between devices with their start and end apart: 19, of which 7 were waited for; matrix products, arithmetic and copies ran while one was open for 0% of the time, Pallas kernels for 19%

profile of v1, /device:TPU:1, one launch (start us, length us, event | category | flops | bytes accessed | tf_op | source)
XLA Modules:
  0.0 61.6 jit_solution(15428109168257532783)
XLA Ops:
  0.6 1.6 %cut_keys.1 = (bf16[64,256]{1,0:T(8,128)(2,1)}, bf16[64,256]{1,0:T(8,128)(2,1)}, bf16[64,256]{1,0:T(8,128)(2,1)}, bf16[64,256]{1,0:T(8,128)(2,1)}) custom-call(bf16[64,512]{1,0:T(8,128)(2,1)} %keys.1, bf16[64,512]{1,0:T(8,128)(2,1)} %values.1), custom_call_target="tpu_custom_call" | custom-call | bytes 262144 | tf_op jit(solution)/shard_map/cut_keys/pallas_call | solution.py:42
  2.2 2.1 %collective-permute-start = (bf16[64,256]{1,0:T(8,128)(2,1)}, bf16[64,256]{1,0:T(8,128)(2,1)S(1)}, u32[]{:S(2)}, u32[]{:S(2)}) collective-permute-start(bf16[64,256]{1,0:T(8,128)(2,1)} %get-tuple-element.56), channel_id=1, source_target_pairs={{0,1},{1,2},{2,3},{3,0},{4,5},{5,6},{6,7},{7,4},{8,9},{9,10},{10,1... | collective-permute-start | bytes 98312 | tf_op jit(solution)/shard_map/ppermute | solution.py:511
  4.3 2.5 %collective-permute-start.1 = (bf16[64,256]{1,0:T(8,128)(2,1)}, bf16[64,256]{1,0:T(8,128)(2,1)S(1)}, u32[]{:S(2)}, u32[]{:S(2)}) collective-permute-start(bf16[64,256]{1,0:T(8,128)(2,1)} %get-tuple-element.57), channel_id=1, source_target_pairs={{0,2},{1,3},{2,0},{3,1},{4,6},{5,7},{6,4},{7,5},{8,10},{9,11},{10,... | collective-permute-start | bytes 98312 | tf_op jit(solution)/shard_map/ppermute | solution.py:511
  6.8 1.2 %collective-permute-start.2 = (bf16[64,256]{1,0:T(8,128)(2,1)}, bf16[64,256]{1,0:T(8,128)(2,1)S(1)}, u32[]{:S(2)}, u32[]{:S(2)}) collective-permute-start(bf16[64,256]{1,0:T(8,128)(2,1)} %get-tuple-element.58), channel_id=1, source_target_pairs={{0,3},{1,0},{2,1},{3,2},{4,7},{5,4},{6,5},{7,6},{8,11},{9,8},{10,9... | collective-permute-start | bytes 98312 | tf_op jit(solution)/shard_map/ppermute | solution.py:511
  8.0 3.8 %mixer_write.1 = (bf16[272,1024]{1,0:T(8,128)(2,1)}, bf16[272,1024]{1,0:T(8,128)(2,1)}, f32[256,32]{1,0:T(8,128)}, f32[32,256]{1,0:T(8,128)}) custom-call(f32[32,256]{1,0:T(8,128)} %bitcast.13, f32[1,32]{1,0:T(1,128)} %bitcast.14, f32[1,32]{1,0:T(1,128)} %bitcast.15, s32[1,256]{1,0:T(1,128)} %bitcast.5, bf16[256,2048]{1,0:T(8,128)(2,1)} %inputs.1, ...), custom_call_target="tpu_custom_call" | custom-call | flops 268435456 | bytes 2393344 | tf_op jit(solution)/shard_map/mixer_write/pallas_call | solution.py:42
  11.9 1.5 %collective-permute-start.3 = (bf16[272,256]{1,0:T(8,128)(2,1)S(1)}, bf16[272,256]{1,0:T(8,128)(2,1)S(1)}, u32[]{:S(2)}, u32[]{:S(2)}) collective-permute-start(bf16[272,256]{1,0:T(8,128)(2,1)S(1)} %assemble_keys.1.mine), channel_id=1, source_target_pairs={{0,4},{4,0},{8,12},{12,8},{16,20},{20,16},{24,28},{28,24},{32,36},... | collective-permute-start | bytes 417800 | tf_op jit(solution)/shard_map/ppermute | solution.py:540
  13.4 1.0 %collective-permute-done.3.other = bf16[272,256]{1,0:T(8,128)(2,1)S(1)} collective-permute-done((bf16[272,256]{1,0:T(8,128)(2,1)S(1)}, bf16[272,256]{1,0:T(8,128)(2,1)S(1)}, u32[]{:S(2)}, u32[]{:S(2)}) %collective-permute-start.3) | collective-permute-done | bytes 139296 | tf_op jit(solution)/shard_map/ppermute | solution.py:540
  14.9 4.8 %collective-permute-start.4 = (bf16[544,256]{1,0:T(8,128)(2,1)S(1)}, bf16[544,256]{1,0:T(8,128)(2,1)S(1)}, u32[]{:S(2)}, u32[]{:S(2)}) collective-permute-start(bf16[544,256]{1,0:T(8,128)(2,1)S(1)} %chunk_keys.1.chunk.chunk_ref), channel_id=1, source_target_pairs={{0,32},{4,68},{8,40},{12,76},{16,48},{20,84},{24,56},{28,92},{32,6... | collective-permute-start | bytes 835592 | tf_op jit(solution)/shard_map/ppermute | solution.py:544
  19.7 1.0 %copy-done.1 = bf16[272,1024]{1,0:T(8,128)(2,1)S(1)} copy-done((bf16[272,1024]{1,0:T(8,128)(2,1)S(1)}, bf16[272,1024]{1,0:T(8,128)(2,1)}, u32[]{:S(2)}) %copy-start.1) | copy-done | bytes 557080
  21.0 1.7 %collective-permute-start.6 = (bf16[272,256]{1,0:T(8,128)(2,1)S(1)}, bf16[272,256]{1,0:T(8,128)(2,1)S(1)}, u32[]{:S(2)}, u32[]{:S(2)}) collective-permute-start(bf16[272,256]{1,0:T(8,128)(2,1)S(1)} %get-tuple-element.74), channel_id=1, source_target_pairs={{0,8},{4,12},{8,16},{12,20},{16,24},{20,28},{24,0},{28,4},{32,40},... | collective-permute-start | bytes 417800 | tf_op jit(solution)/shard_map/ppermute | solution.py:548
  22.7 3.3 %collective-permute-start.7 = (bf16[272,256]{1,0:T(8,128)(2,1)S(1)}, bf16[272,256]{1,0:T(8,128)(2,1)S(1)}, u32[]{:S(2)}, u32[]{:S(2)}) collective-permute-start(bf16[272,256]{1,0:T(8,128)(2,1)S(1)} %get-tuple-element.75), channel_id=1, source_target_pairs={{0,16},{4,20},{8,24},{12,28},{16,0},{20,4},{24,8},{28,12},{32,48},... | collective-permute-start | bytes 417800 | tf_op jit(solution)/shard_map/ppermute | solution.py:548
  27.6 2.1 %mixer_inside.1.inside = f32[256,2048]{1,0:T(8,128)S(1)} custom-call(f32[256,32]{1,0:T(8,128)S(1)} %copy-done.4, f32[32,256]{1,0:T(8,128)S(1)} %copy-done.6, s32[1,256]{1,0:T(1,128)S(1)} %bitcast.7, bf16[256,2048]{1,0:T(8,128)(2,1)S(1)} %copy-done, bf16[256,256]{1,0:T(8,128)(2,1)S(1)} %copy-done.5, bf16[256,256]{1,0:T(8,128)(2,1)S(1)} %copy-done.3, ...), custom_call_target="tpu_custom_call" | custom-call | flops 536870912 | bytes 3474560 | tf_op jit(solution)/shard_map/mixer_inside/pallas_call | solution.py:42
  31.1 2.0 %collective-permute-start.16 = (bf16[544,256]{1,0:T(8,128)(2,1)S(1)}, bf16[544,256]{1,0:T(8,128)(2,1)S(1)}, u32[]{:S(2)}, u32[]{:S(2)}) collective-permute-start(bf16[544,256]{1,0:T(8,128)(2,1)S(1)} %get-tuple-element.81), channel_id=1, source_target_pairs={{0,24},{4,28},{8,0},{12,4},{16,8},{20,12},{24,16},{28,20},{32,56},... | collective-permute-start | bytes 835592 | tf_op jit(solution)/shard_map/ppermute | solution.py:567
  33.4 3.5 %collective-permute-start.10 = (bf16[272,256]{1,0:T(8,128)(2,1)S(1)}, bf16[272,256]{1,0:T(8,128)(2,1)S(1)}, u32[]{:S(2)}, u32[]{:S(2)}) collective-permute-start(bf16[272,256]{1,0:T(8,128)(2,1)S(1)} %row_state.1), channel_id=1, source_target_pairs={{0,64},{4,68},{8,72},{12,76},{16,80},{20,84},{24,88},{28,92},{32,9... | collective-permute-start | bytes 417800 | tf_op jit(solution)/shard_map/ppermute | solution.py:572
  36.9 1.3 %collective-permute-start.9 = (bf16[272,256]{1,0:T(8,128)(2,1)S(1)}, bf16[272,256]{1,0:T(8,128)(2,1)S(1)}, u32[]{:S(2)}, u32[]{:S(2)}) collective-permute-start(bf16[272,256]{1,0:T(8,128)(2,1)S(1)} %row_state.1), channel_id=1, source_target_pairs={{0,32},{4,36},{8,40},{12,44},{16,48},{20,52},{24,56},{28,60},{32,6... | collective-permute-start | bytes 417800 | tf_op jit(solution)/shard_map/ppermute | solution.py:571
  38.2 1.8 %attention_own.1 = (bf16[8,256,256]{2,1,0:T(8,128)(2,1)S(1)}, f32[8,256]{1,0:T(8,128)S(1)}, f32[8,144,256]{2,1,0:T(8,128)S(1)}) custom-call(bf16[256,1024]{1,0:T(8,128)(2,1)S(1)} %copy-done.10, s32[1,256]{1,0:T(1,128)S(1)} %bitcast.8, bf16[544,256]{1,0:T(8,128)(2,1)S(1)} %chunk_keys.1.chunk.chunk_ref), custom_call_target="tpu_custom_call" | custom-call | flops 536870912 | bytes 3040256 | tf_op jit(solution)/shard_map/attention_own/pallas_call | solution.py:42
  40.0 1.6 %collective-permute-done.9.near = bf16[272,256]{1,0:T(8,128)(2,1)S(1)} collective-permute-done((bf16[272,256]{1,0:T(8,128)(2,1)S(1)}, bf16[272,256]{1,0:T(8,128)(2,1)S(1)}, u32[]{:S(2)}, u32[]{:S(2)}) %collective-permute-start.9) | collective-permute-done | bytes 139296 | tf_op jit(solution)/shard_map/ppermute | solution.py:571
  41.9 3.7 %collective-permute-done.14.a1 = bf16[544,256]{1,0:T(8,128)(2,1)S(1)} collective-permute-done((bf16[544,256]{1,0:T(8,128)(2,1)S(1)}, bf16[544,256]{1,0:T(8,128)(2,1)S(1)}, u32[]{:S(2)}, u32[]{:S(2)}) %collective-permute-start.14) | collective-permute-done | bytes 278560 | tf_op jit(solution)/shard_map/ppermute | solution.py:567
  47.5 3.0 %collective-permute-start.12 = (bf16[272,256]{1,0:T(8,128)(2,1)S(1)}, bf16[272,256]{1,0:T(8,128)(2,1)S(1)}, u32[]{:S(2)}, u32[]{:S(2)}) collective-permute-start(bf16[272,256]{1,0:T(8,128)(2,1)S(1)} %get-tuple-element.91), channel_id=1, source_target_pairs={{0,16},{4,20},{8,24},{12,28},{16,0},{20,4},{24,8},{28,12},{32,48},... | collective-permute-start | bytes 417800 | tf_op jit(solution)/shard_map/ppermute | solution.py:590
  50.5 1.9 %attention.1 = bf16[256,1024]{1,0:T(8,128)(2,1)} custom-call(s32[1,256]{1,0:T(1,128)S(1)} %bitcast.9, bf16[544,256]{1,0:T(8,128)(2,1)S(1)} %chunk_keys.1.chunk.chunk_ref, bf16[2176,256]{1,0:T(8,128)(2,1)S(1)} %bundle_keys.1.bundle, bf16[2176,256]{1,0:T(8,128)(2,1)S(1)} %collective-permute-done.17.arrived, bf16[8,256,256]{2,1,0:T(8,128)(2,1)S(1)} %get-tuple-element.96.turned, ...), custom_call_target="tpu_custom_call" | custom-call | flops 4294967296 | bytes 5268480 | tf_op jit(solution)/shard_map/attention/pallas_call | solution.py:42
  52.4 1.0 %collective-permute-done.11.b1 = bf16[272,256]{1,0:T(8,128)(2,1)S(1)} collective-permute-done((bf16[272,256]{1,0:T(8,128)(2,1)S(1)}, bf16[272,256]{1,0:T(8,128)(2,1)S(1)}, u32[]{:S(2)}, u32[]{:S(2)}) %collective-permute-start.11) | collective-permute-done | bytes 139296 | tf_op jit(solution)/shard_map/ppermute | solution.py:590
  53.4 3.8 %collective-permute-done.12.b2 = bf16[272,256]{1,0:T(8,128)(2,1)S(1)} collective-permute-done((bf16[272,256]{1,0:T(8,128)(2,1)S(1)}, bf16[272,256]{1,0:T(8,128)(2,1)S(1)}, u32[]{:S(2)}, u32[]{:S(2)}) %collective-permute-start.12) | collective-permute-done | bytes 139296 | tf_op jit(solution)/shard_map/ppermute | solution.py:590
  58.6 1.3 %mixer_carried_own.1.refs_0_ = bf16[256,2048]{1,0:T(8,128)(2,1)} custom-call(f32[256,2048]{1,0:T(8,128)S(1)} %mixer_inside.1.inside, f32[256,32]{1,0:T(8,128)S(1)} %copy-done.4, s32[1,256]{1,0:T(1,128)S(1)} %bitcast.10, bf16[256,256]{1,0:T(8,128)(2,1)S(1)} %copy-done.3, bf16[272,1024]{1,0:T(8,128)(2,1)S(1)} %get-tuple-element.103.keep.state, ...), custom_call_target="tpu_custom_call" | custom-call | flops 134217728 | bytes 4424704 | tf_op jit(solution)/shard_map/mixer_carried_own/pallas_call | solution.py:42
  60.1 1.3 %mixer_carried.1 = bf16[256,2048]{1,0:T(8,128)(2,1)} custom-call(f32[256,2048]{1,0:T(8,128)S(1)} %mixer_inside.1.inside, f32[256,32]{1,0:T(8,128)S(1)} %copy-done.4, s32[1,256]{1,0:T(1,128)S(1)} %bitcast.11, bf16[256,256]{1,0:T(8,128)(2,1)S(1)} %copy-done.3, bf16[272,1024]{1,0:T(8,128)(2,1)S(1)} %get-tuple-element.103.keep.state, ...), custom_call_target="tpu_custom_call", output_to_operand_aliasing={{}: (6, {})} | custom-call | flops 134217728 | bytes 5473280 | tf_op jit(solution)/shard_map/mixer_carried/pallas_call | solution.py:42
  (51 shorter events, 7.7 us)
Async XLA Ops:
  0.6 11.1 %copy-start.8 = (s32[256]{0:T(256)S(1)}, s32[256]{0:T(256)}, u32[]{:S(2)}) copy-start(s32[256]{0:T(256)} %param.18) | copy-start | bytes 3076
  2.2 9.5 %collective-permute-start = (bf16[64,256]{1,0:T(8,128)(2,1)}, bf16[64,256]{1,0:T(8,128)(2,1)S(1)}, u32[]{:S(2)}, u32[]{:S(2)}) collective-permute-start(bf16[64,256]{1,0:T(8,128)(2,1)} %get-tuple-element.56), channel_id=1, source_target_pairs={{0,1},{1,2},{2,3},{3,0},{4,5},{5,6},{6,7},{7,4},{8,9},{9,10},{10,1... | collective-permute-start | bytes 98312 | tf_op jit(solution)/shard_map/ppermute | solution.py:511
  4.3 7.4 %collective-permute-start.1 = (bf16[64,256]{1,0:T(8,128)(2,1)}, bf16[64,256]{1,0:T(8,128)(2,1)S(1)}, u32[]{:S(2)}, u32[]{:S(2)}) collective-permute-start(bf16[64,256]{1,0:T(8,128)(2,1)} %get-tuple-element.57), channel_id=1, source_target_pairs={{0,2},{1,3},{2,0},{3,1},{4,6},{5,7},{6,4},{7,5},{8,10},{9,11},{10,... | collective-permute-start | bytes 98312 | tf_op jit(solution)/shard_map/ppermute | solution.py:511
  6.8 5.0 %collective-permute-start.2 = (bf16[64,256]{1,0:T(8,128)(2,1)}, bf16[64,256]{1,0:T(8,128)(2,1)S(1)}, u32[]{:S(2)}, u32[]{:S(2)}) collective-permute-start(bf16[64,256]{1,0:T(8,128)(2,1)} %get-tuple-element.58), channel_id=1, source_target_pairs={{0,3},{1,0},{2,1},{3,2},{4,7},{5,4},{6,5},{7,6},{8,11},{9,8},{10,9... | collective-permute-start | bytes 98312 | tf_op jit(solution)/shard_map/ppermute | solution.py:511
  7.9 18.8 %copy-start.3 = (bf16[256,256]{1,0:T(8,128)(2,1)S(1)}, bf16[256,256]{1,0:T(8,128)(2,1)}, u32[]{:S(2)}) copy-start(bf16[256,256]{1,0:T(8,128)(2,1)} %reads.5) | copy-start | bytes 393220
  7.9 18.8 %copy-start.5 = (bf16[256,256]{1,0:T(8,128)(2,1)S(1)}, bf16[256,256]{1,0:T(8,128)(2,1)}, u32[]{:S(2)}) copy-start(bf16[256,256]{1,0:T(8,128)(2,1)} %writes.1) | copy-start | bytes 393220
  8.0 18.8 %copy-start.9 = (f32[32]{0:T(128)S(1)}, f32[32]{0:T(128)}, u32[]{:S(2)}) copy-start(f32[32]{0:T(128)} %param.15) | copy-start | bytes 388
  11.7 15.1 %copy-start = (bf16[256,2048]{1,0:T(8,128)(2,1)S(1)}, bf16[256,2048]{1,0:T(8,128)(2,1)}, u32[]{:S(2)}) copy-start(bf16[256,2048]{1,0:T(8,128)(2,1)} %inputs.1) | copy-start | bytes 3145732
  11.9 2.5 %collective-permute-start.3 = (bf16[272,256]{1,0:T(8,128)(2,1)S(1)}, bf16[272,256]{1,0:T(8,128)(2,1)S(1)}, u32[]{:S(2)}, u32[]{:S(2)}) collective-permute-start(bf16[272,256]{1,0:T(8,128)(2,1)S(1)} %assemble_keys.1.mine), channel_id=1, source_target_pairs={{0,4},{4,0},{8,12},{12,8},{16,20},{20,16},{24,28},{28,24},{32,36},... | collective-permute-start | bytes 417800 | tf_op jit(solution)/shard_map/ppermute | solution.py:540
  14.5 5.3 %collective-permute-start.5 = (bf16[272,1024]{1,0:T(8,128)(2,1)}, bf16[272,1024]{1,0:T(8,128)(2,1)S(1)}, u32[]{:S(2)}, u32[]{:S(2)}) collective-permute-start(bf16[272,1024]{1,0:T(8,128)(2,1)} %get-tuple-element.72), channel_id=1, source_target_pairs={{0,4},{4,0},{8,12},{12,8},{16,20},{20,16},{24,28},{28,24},{32,36},... | collective-permute-start | bytes 1671176 | tf_op jit(solution)/shard_map/ppermute | solution.py:546
  14.9 14.8 %collective-permute-start.4 = (bf16[544,256]{1,0:T(8,128)(2,1)S(1)}, bf16[544,256]{1,0:T(8,128)(2,1)S(1)}, u32[]{:S(2)}, u32[]{:S(2)}) collective-permute-start(bf16[544,256]{1,0:T(8,128)(2,1)S(1)} %chunk_keys.1.chunk.chunk_ref), channel_id=1, source_target_pairs={{0,32},{4,68},{8,40},{12,76},{16,48},{20,84},{24,56},{28,92},{32,6... | collective-permute-start | bytes 835592 | tf_op jit(solution)/shard_map/ppermute | solution.py:544
  21.0 10.1 %collective-permute-start.6 = (bf16[272,256]{1,0:T(8,128)(2,1)S(1)}, bf16[272,256]{1,0:T(8,128)(2,1)S(1)}, u32[]{:S(2)}, u32[]{:S(2)}) collective-permute-start(bf16[272,256]{1,0:T(8,128)(2,1)S(1)} %get-tuple-element.74), channel_id=1, source_target_pairs={{0,8},{4,12},{8,16},{12,20},{16,24},{20,28},{24,0},{28,4},{32,40},... | collective-permute-start | bytes 417800 | tf_op jit(solution)/shard_map/ppermute | solution.py:548
  22.7 10.4 %collective-permute-start.7 = (bf16[272,256]{1,0:T(8,128)(2,1)S(1)}, bf16[272,256]{1,0:T(8,128)(2,1)S(1)}, u32[]{:S(2)}, u32[]{:S(2)}) collective-permute-start(bf16[272,256]{1,0:T(8,128)(2,1)S(1)} %get-tuple-element.75), channel_id=1, source_target_pairs={{0,16},{4,20},{8,24},{12,28},{16,0},{20,4},{24,8},{28,12},{32,48},... | collective-permute-start | bytes 417800 | tf_op jit(solution)/shard_map/ppermute | solution.py:548
  26.0 7.1 %collective-permute-start.8 = (bf16[272,256]{1,0:T(8,128)(2,1)S(1)}, bf16[272,256]{1,0:T(8,128)(2,1)S(1)}, u32[]{:S(2)}, u32[]{:S(2)}) collective-permute-start(bf16[272,256]{1,0:T(8,128)(2,1)S(1)} %get-tuple-element.76), channel_id=1, source_target_pairs={{0,24},{4,28},{8,0},{12,4},{16,8},{20,12},{24,16},{28,20},{32,56},... | collective-permute-start | bytes 417800 | tf_op jit(solution)/shard_map/ppermute | solution.py:548
  29.9 15.8 %collective-permute-start.14 = (bf16[544,256]{1,0:T(8,128)(2,1)S(1)}, bf16[544,256]{1,0:T(8,128)(2,1)S(1)}, u32[]{:S(2)}, u32[]{:S(2)}) collective-permute-start(bf16[544,256]{1,0:T(8,128)(2,1)S(1)} %get-tuple-element.79), channel_id=1, source_target_pairs={{0,8},{4,12},{8,16},{12,20},{16,24},{20,28},{24,0},{28,4},{32,40},... | collective-permute-start | bytes 835592 | tf_op jit(solution)/shard_map/ppermute | solution.py:567
  30.7 15.0 %collective-permute-start.15 = (bf16[544,256]{1,0:T(8,128)(2,1)S(1)}, bf16[544,256]{1,0:T(8,128)(2,1)S(1)}, u32[]{:S(2)}, u32[]{:S(2)}) collective-permute-start(bf16[544,256]{1,0:T(8,128)(2,1)S(1)} %get-tuple-element.80), channel_id=1, source_target_pairs={{0,16},{4,20},{8,24},{12,28},{16,0},{20,4},{24,8},{28,12},{32,48},... | collective-permute-start | bytes 835592 | tf_op jit(solution)/shard_map/ppermute | solution.py:567
  31.1 15.0 %collective-permute-start.16 = (bf16[544,256]{1,0:T(8,128)(2,1)S(1)}, bf16[544,256]{1,0:T(8,128)(2,1)S(1)}, u32[]{:S(2)}, u32[]{:S(2)}) collective-permute-start(bf16[544,256]{1,0:T(8,128)(2,1)S(1)} %get-tuple-element.81), channel_id=1, source_target_pairs={{0,24},{4,28},{8,0},{12,4},{16,8},{20,12},{24,16},{28,20},{32,56},... | collective-permute-start | bytes 835592 | tf_op jit(solution)/shard_map/ppermute | solution.py:567
  33.4 6.6 %collective-permute-start.10 = (bf16[272,256]{1,0:T(8,128)(2,1)S(1)}, bf16[272,256]{1,0:T(8,128)(2,1)S(1)}, u32[]{:S(2)}, u32[]{:S(2)}) collective-permute-start(bf16[272,256]{1,0:T(8,128)(2,1)S(1)} %row_state.1), channel_id=1, source_target_pairs={{0,64},{4,68},{8,72},{12,76},{16,80},{20,84},{24,88},{28,92},{32,9... | collective-permute-start | bytes 417800 | tf_op jit(solution)/shard_map/ppermute | solution.py:572
  36.9 4.7 %collective-permute-start.9 = (bf16[272,256]{1,0:T(8,128)(2,1)S(1)}, bf16[272,256]{1,0:T(8,128)(2,1)S(1)}, u32[]{:S(2)}, u32[]{:S(2)}) collective-permute-start(bf16[272,256]{1,0:T(8,128)(2,1)S(1)} %row_state.1), channel_id=1, source_target_pairs={{0,32},{4,36},{8,40},{12,44},{16,48},{20,52},{24,56},{28,60},{32,6... | collective-permute-start | bytes 417800 | tf_op jit(solution)/shard_map/ppermute | solution.py:571
  46.2 4.3 %collective-permute-start.17 = (bf16[2176,256]{1,0:T(8,128)(2,1)S(1)}, bf16[2176,256]{1,0:T(8,128)(2,1)S(1)}, u32[]{:S(2)}, u32[]{:S(2)}) collective-permute-start(bf16[2176,256]{1,0:T(8,128)(2,1)S(1)} %bundle_keys.1.bundle), channel_id=1, source_target_pairs={{0,4},{4,0},{8,12},{12,8},{16,20},{20,16},{24,28},{28,24},{32,36},... | collective-permute-start | bytes 3342344 | tf_op jit(solution)/shard_map/ppermute | solution.py:594
  47.0 6.5 %collective-permute-start.11 = (bf16[272,256]{1,0:T(8,128)(2,1)S(1)}, bf16[272,256]{1,0:T(8,128)(2,1)S(1)}, u32[]{:S(2)}, u32[]{:S(2)}) collective-permute-start(bf16[272,256]{1,0:T(8,128)(2,1)S(1)} %get-tuple-element.90), channel_id=1, source_target_pairs={{0,8},{4,12},{8,16},{12,20},{16,24},{20,28},{24,0},{28,4},{32,40},... | collective-permute-start | bytes 417800 | tf_op jit(solution)/shard_map/ppermute | solution.py:590
  47.5 9.8 %collective-permute-start.12 = (bf16[272,256]{1,0:T(8,128)(2,1)S(1)}, bf16[272,256]{1,0:T(8,128)(2,1)S(1)}, u32[]{:S(2)}, u32[]{:S(2)}) collective-permute-start(bf16[272,256]{1,0:T(8,128)(2,1)S(1)} %get-tuple-element.91), channel_id=1, source_target_pairs={{0,16},{4,20},{8,24},{12,28},{16,0},{20,4},{24,8},{28,12},{32,48},... | collective-permute-start | bytes 417800 | tf_op jit(solution)/shard_map/ppermute | solution.py:590
  50.5 6.7 %collective-permute-start.13 = (bf16[272,256]{1,0:T(8,128)(2,1)S(1)}, bf16[272,256]{1,0:T(8,128)(2,1)S(1)}, u32[]{:S(2)}, u32[]{:S(2)}) collective-permute-start(bf16[272,256]{1,0:T(8,128)(2,1)S(1)} %get-tuple-element.92), channel_id=1, source_target_pairs={{0,24},{4,28},{8,0},{12,4},{16,8},{20,12},{24,16},{28,20},{32,56},... | collective-permute-start | bytes 417800 | tf_op jit(solution)/shard_map/ppermute | solution.py:590
  57.6 2.5 %collective-permute-start.18 = (bf16[272,1024]{1,0:T(8,128)(2,1)S(1)}, bf16[272,1024]{1,0:T(8,128)(2,1)S(1)}, u32[]{:S(2)}, u32[]{:S(2)}) collective-permute-start(bf16[272,1024]{1,0:T(8,128)(2,1)S(1)} %get-tuple-element.104), channel_id=1, source_target_pairs={{0,4},{4,0},{8,12},{12,8},{16,20},{20,16},{24,28},{28,24},{32,36},... | collective-permute-start | bytes 1671176 | tf_op jit(solution)/shard_map/ppermute | solution.py:618
  (6 other events, 32.6 us)
